TPU v7x, 128 devices: a whole 4x4x4 slice. The times are simulated.
128 devices in a mesh: ex: 8 (over y_hi, x), ey: 4 (over y_lo, core), dp: 4 (over z).
Axes of the slice: x: 4, y: 4 (y_hi: 2, y_lo: 2; y = y_hi * 2 + y_lo), z: 4, core: 2. Of those that a mesh axis runs over, the one named last changes fastest.
Arguments:
- tokens: bfloat16 [2048, 2048], P(('ex', 'ey', 'dp')), may hold values from -6 to 6
- cotangent: bfloat16 [2048, 2048], P(('ex', 'ey', 'dp')), may hold values from -1.796875 to 1.796875
- route_weights: float32 [2048, 2], P(('ex', 'ey', 'dp')), may hold values from 0.2 to 1
- expert_ids: int32 [2048, 2], P(('ex', 'ey', 'dp')), may hold values from 0 to 15, as said below
- slot_ids: int32 [2048, 2], P(('ex', 'ey', 'dp')), may hold values from -1 to 1, as said below
- gate_weight: bfloat16 [16, 2048, 8192], P('ex', None, ('ey', 'dp')), may hold values from -0.125 to 0.125
- up_weight: bfloat16 [16, 2048, 8192], P('ex', None, ('ey', 'dp')), may hold values from -0.125 to 0.125
- down_weight: bfloat16 [16, 8192, 2048], P('ex', ('ey', 'dp')), may hold values from -0.0625 to 0.0625
Outputs:
- grad_tokens: bfloat16 [2048, 2048], P(('ex', 'ey', 'dp'))
- grad_gate: bfloat16 [16, 2048, 8192], P('ex', None, ('ey', 'dp'))
- grad_up: bfloat16 [16, 2048, 8192], P('ex', None, ('ey', 'dp'))
- grad_down: bfloat16 [16, 8192, 2048], P('ex', ('ey', 'dp'))
Inputs may be any that keep to these rules, and one draw needn't show every extreme that they name: `expert_ids`: each token names 2 different experts. `slot_ids`: within the tokens of one device, the choices that name one expert, taken in order of token and then of choice, hold slots 0, 1, 2 and so on; those past 2 of them hold -1. In every draw some expert is given 2 rows by every device.
All inputs are finite; a program needn't handle non-finite values.
Results may differ from a plain program's by a relative error of at most 0.0058.
Values may be sent and summed in bfloat16 or wider, within the bound.
A program may use at most 128 MiB of HBM per device.

v0:
```python
import jax
import jax.numpy as jnp
from jax import lax
from jax.sharding import PartitionSpec as P


def smooth(argument):
    return jax.nn.gelu(argument, approximate=True)


def per_device(
    tokens, cotangent, route_weights, expert_ids, slot_ids, gate_weight, up_weight, down_weight
):
    ex_count = lax.axis_size("ex")
    shards = lax.axis_size(("ey", "dp"))
    local_count = gate_weight.shape[0]
    experts = ex_count * local_count
    tok_count, top_count = expert_ids.shape
    model_width = tokens.shape[1]
    hidden_count = gate_weight.shape[2]
    capacity = min(tok_count * top_count * 5 // (4 * experts), tok_count - 1)
    cell_count = experts * capacity
    target = jnp.where(slot_ids >= 0, expert_ids * capacity + slot_ids, -1)
    cell_iota = lax.broadcasted_iota(jnp.int32, (cell_count, tok_count, top_count), 0)
    token_iota = lax.broadcasted_iota(jnp.int32, (cell_count, tok_count, top_count), 1)
    matches = cell_iota == target[None]
    cell_token = jnp.sum(jnp.where(matches, token_iota, 0), axis=(1, 2))
    cell_scale = jnp.sum(jnp.where(matches, route_weights[None], 0.0), axis=(1, 2))
    cell_live = jnp.any(matches, axis=(1, 2))
    send_input = jnp.where(cell_live[:, None], tokens[cell_token], jnp.zeros((), jnp.bfloat16))
    send_input = send_input.reshape(ex_count, local_count, capacity, model_width)
    send_grad = (cell_scale[:, None] * cotangent[cell_token].astype(jnp.float32)).astype(
        jnp.bfloat16
    )
    send_grad = send_grad.reshape(ex_count, local_count, capacity, model_width)
    block_rows = ex_count * capacity
    total_rows = shards * block_rows
    rows_input, rows_grad = (
        lax.all_to_all(
            jnp.repeat(send_input, shards, axis=0),
            ("ex", "ey", "dp"),
            split_axis=0,
            concat_axis=0,
            tiled=True,
        ),
        lax.all_to_all(
            jnp.repeat(send_grad, shards, axis=0),
            ("ex", "ey", "dp"),
            split_axis=0,
            concat_axis=0,
            tiled=True,
        ),
    )
    rows_input = jnp.transpose(rows_input, (1, 0, 2, 3)).reshape(
        local_count, total_rows, model_width
    )
    rows_grad = jnp.transpose(rows_grad, (1, 0, 2, 3)).reshape(local_count, total_rows, model_width)
    weight_pair = jnp.concatenate([gate_weight, up_weight], axis=2)
    pre_pair = jnp.einsum(
        "jrd,jdf->jrf", rows_input, weight_pair, preferred_element_type=jnp.float32
    )
    pre_gate = pre_pair[:, :, :hidden_count]
    pre_up = pre_pair[:, :, hidden_count:]
    activated, backward = jax.vjp(smooth, pre_gate)
    hidden = (activated * pre_up).astype(jnp.bfloat16)
    grad_hidden = jnp.einsum(
        "jrd,jfd->jrf", rows_grad, down_weight, preferred_element_type=jnp.float32
    )
    grad_up_rows = (grad_hidden * activated).astype(jnp.bfloat16)
    grad_gate_rows = backward(grad_hidden * pre_up)[0].astype(jnp.bfloat16)
    grad_pair = jnp.concatenate([grad_gate_rows, grad_up_rows], axis=2)
    grad_both = jnp.einsum(
        "jrd,jrf->jdf", rows_input, grad_pair, preferred_element_type=jnp.float32
    )
    grad_down = jnp.einsum("jrf,jrd->jfd", hidden, rows_grad, preferred_element_type=jnp.float32)
    partial_all = jnp.einsum(
        "jrf,jdf->rjd", grad_pair, weight_pair, preferred_element_type=jnp.float32
    )
    partial_all = partial_all.reshape(ex_count * shards, capacity, local_count, model_width)
    partial_all = jnp.transpose(partial_all, (0, 2, 1, 3))
    arrived = lax.all_to_all(
        partial_all, ("ex", "ey", "dp"), split_axis=0, concat_axis=0, tiled=True
    )
    returned = jnp.sum(
        arrived.reshape(ex_count, shards, local_count, capacity, model_width), axis=1
    )
    returned_cells = returned.reshape(cell_count, model_width)
    picked = returned_cells[jnp.maximum(target, 0)]
    grad_tokens = jnp.sum(jnp.where((target >= 0)[:, :, None], picked, 0.0), axis=1).astype(
        jnp.bfloat16
    )
    grad_gate = grad_both[:, :, :hidden_count].astype(jnp.bfloat16)
    grad_up = grad_both[:, :, hidden_count:].astype(jnp.bfloat16)
    return (grad_tokens, grad_gate, grad_up, grad_down.astype(jnp.bfloat16))


def solution(mesh):
    return jax.shard_map(
        per_device,
        mesh=mesh,
        in_specs=(
            P(("ex", "ey", "dp"), None),
            P(("ex", "ey", "dp"), None),
            P(("ex", "ey", "dp"), None),
            P(("ex", "ey", "dp"), None),
            P(("ex", "ey", "dp"), None),
            P("ex", None, ("ey", "dp")),
            P("ex", None, ("ey", "dp")),
            P("ex", ("ey", "dp"), None),
        ),
        out_specs=(
            P(("ex", "ey", "dp"), None),
            P("ex", None, ("ey", "dp")),
            P("ex", None, ("ey", "dp")),
            P("ex", ("ey", "dp"), None),
        ),
        check_vma=False,
    )
```

profile of v0, /device:TPU:0, one launch (start us, length us, event | category | flops | bytes accessed | tf_op | source)
XLA Modules:
  0.0 186.8 jit_solution(2987391680513729178)
XLA Ops:
  0.6 0.0 copy-start
  0.6 0.7 broadcast_compare_fusion
  1.4 0.1 select_reduce_fusion.1
  1.5 0.8 select_reduce_fusion.2
  2.3 0.1 mul.72
  2.4 0.0 copy-start.2
  2.4 0.7 gather_fusion
  3.0 0.2 reshape.70
  3.2 0.2 multiply_convert_fusion.3
  3.4 3.4 %broadcast_in_dim.67 = bf16[8,16,2,2,2048]{4,3,2,1,0:T(2,128)(2,1)} broadcast(bf16[8,2,2,2048]{3,2,1,0:T(2,128)(2,1)S(1)} %multiply_convert_fusion.3), dimensions={0,2,3,4} | broadcast | bytes 2228224 | tf_op jit(solution)/shard_map/broadcast_in_dim | solution.py:47
  6.8 11.1 %all-to-all-start = ((bf16[128,2,2,2048]{3,2,1,0:T(2,128)(2,1)}), bf16[128,2,2,2048]{3,2,1,0:T(2,128)(2,1)S(1)}, u32[]{:S(2)}, u32[]{:S(2)}) async-start(bf16[128,2,2,2048]{3,2,1,0:T(2,128)(2,1)} %bitcast.26), calls=%async_computation | async-start | bytes 4194304 | tf_op jit(solution)/shard_map/all_to_all | solution.py:46
  17.9 0.1 fusion.7
  18.0 0.1 broadcast_in_dim.68
  18.1 0.7 gather_fusion.1
  18.8 0.1 gather.13
  18.9 0.2 broadcast_select_fusion
  19.1 29.1 %all-to-all-done = bf16[128,2,2,2048]{3,2,1,0:T(2,128)(2,1)S(1)} async-done(((bf16[128,2,2,2048]{3,2,1,0:T(2,128)(2,1)}), bf16[128,2,2,2048]{3,2,1,0:T(2,128)(2,1)S(1)}, u32[]{:S(2)}, u32[]{:S(2)}) %all-to-all-start) | async-done | bytes 2097184 | tf_op jit(solution)/shard_map/all_to_all | solution.py:46
  48.2 3.4 %broadcast_in_dim.71 = bf16[8,16,2,2,2048]{4,3,2,1,0:T(2,128)(2,1)} broadcast(bf16[8,2,2,2048]{3,2,1,0:T(2,128)(2,1)S(1)} %broadcast_select_fusion), dimensions={0,2,3,4} | broadcast | bytes 2228224 | tf_op jit(solution)/shard_map/broadcast_in_dim | solution.py:40
  51.6 6.0 %all-to-all-start.1 = ((bf16[128,2,2,2048]{3,2,1,0:T(2,128)(2,1)}), bf16[128,2,2,2048]{3,2,1,0:T(2,128)(2,1)}, u32[]{:S(2)}, u32[]{:S(2)}) async-start(bf16[128,2,2,2048]{3,2,1,0:T(2,128)(2,1)} %bitcast.27), calls=%async_computation.1 | async-start | bytes 4194304 | tf_op jit(solution)/shard_map/all_to_all | solution.py:39
  57.6 0.0 copy-start.5
  57.6 4.7 %constant_dynamic-update-slice_fusion.1 = bf16[2,2048,1024]{2,1,0:T(8,128)(2,1)} fusion(bf16[2,2048,512]{2,1,0:T(8,128)(2,1)} %param.13), kind=kLoop, calls=%fused_computation.31 | loop fusion | bytes 8388608
  62.3 2.4 %constant_dynamic-update-slice_fusion = bf16[2,2048,1024]{2,1,0:T(8,128)(2,1)} fusion(bf16[2,2048,1024]{2,1,0:T(8,128)(2,1)} %constant_dynamic-update-slice_fusion.1, bf16[2,2048,512]{2,1,0:T(8,128)(2,1)S(1)} %copy-done.5), kind=kLoop, calls=%fused_computation.30 | loop fusion | bytes 8388608 | tf_op jit(solution)/shard_map/concatenate | solution.py:58
  64.6 2.8 %copy.40 = bf16[2,128,2,2048]{3,2,1,0:T(2,128)(2,1)} copy(bf16[2,128,2,2048]{3,2,0,1:T(2,128)(2,1)S(1)} %bitcast.25) | data formatting | bytes 4194304 | tf_op jit(solution)/shard_map/transpose | solution.py:57
  67.4 4.1 %reshape.64 = bf16[2,256,2048]{2,1,0:T(8,128)(2,1)} reshape(bf16[2,128,2,2048]{3,2,1,0:T(2,128)(2,1)} %copy.40) | data formatting | bytes 4194304 | tf_op jit(solution)/shard_map/reshape | solution.py:57
  71.5 15.7 %all-to-all-done.1 = bf16[128,2,2,2048]{3,2,1,0:T(2,128)(2,1)} async-done(((bf16[128,2,2,2048]{3,2,1,0:T(2,128)(2,1)}), bf16[128,2,2,2048]{3,2,1,0:T(2,128)(2,1)}, u32[]{:S(2)}, u32[]{:S(2)}) %all-to-all-start.1) | async-done | bytes 2097184 | tf_op jit(solution)/shard_map/all_to_all | solution.py:39
  87.2 4.3 %copy.41 = bf16[2,128,2,2048]{3,2,1,0:T(2,128)(2,1)} copy(bf16[2,128,2,2048]{3,2,0,1:T(2,128)(2,1)} %bitcast.5) | data formatting | bytes 4194304 | tf_op jit(solution)/shard_map/transpose | solution.py:54
  91.6 2.7 %reshape.66 = bf16[2,256,2048]{2,1,0:T(8,128)(2,1)S(1)} reshape(bf16[2,128,2,2048]{3,2,1,0:T(2,128)(2,1)} %copy.41) | data formatting | bytes 4194304 | tf_op jit(solution)/shard_map/reshape | solution.py:54
  94.3 0.0 copy-start.4
  94.3 0.0 copy-start.6
  94.4 5.9 %fusion.16 = f32[2,256,1024]{2,1,0:T(8,128)S(1)} fusion(bf16[2,256,2048]{2,1,0:T(8,128)(2,1)S(1)} %reshape.66, bf16[2,2048,1024]{2,1,0:T(8,128)(2,1)} %constant_dynamic-update-slice_fusion), kind=kOutput, calls=%fused_computation.44 | convolution fusion | flops 2147483648 | bytes 12582912 | tf_op jit(solution)/shard_map/jrd,jdf->jrf/dot_general | solution.py:59
  100.2 2.0 %fusion.6 = (bf16[2,256,512]{2,1,0:T(8,128)(2,1)S(1)}, bf16[2,256,512]{2,1,0:T(8,128)(2,1)S(1)}) fusion(f32[2,256,1024]{2,1,0:T(8,128)S(1)} %fusion.16, bf16[2,256,2048]{2,1,0:T(8,128)(2,1)S(1)} %copy-done.4, bf16[2,512,2048]{2,1,0:T(8,128)(2,1)S(1)} %copy-done.6), kind=kOutput, calls=%fused_computation.16 | convolution fusion | flops 1080033280 | bytes 9437184 | tf_op jit(solution)/shard_map/jrd,jfd->jrf/dot_general | solution.py:66
  102.3 7.8 %convolution_bitcast_fusion = f32[256,2,2048]{2,0,1:T(8,128)} fusion(bf16[2,2048,1024]{2,1,0:T(8,128)(2,1)} %constant_dynamic-update-slice_fusion, bf16[2,256,512]{2,1,0:T(8,128)(2,1)S(1)} %get-tuple-element.9, bf16[2,256,512]{2,1,0:T(8,128)(2,1)S(1)} %get-tuple-element.8), kind=kOutput, calls=%fused_computation.7 | convolution fusion | flops 2149580800 | bytes 13631488 | tf_op jit(solution)/shard_map/jrf,jdf->rjd/dot_general | solution.py:76
  110.0 5.8 %reshape.67 = f32[128,2,2,2048]{3,1,0,2:T(2,128)} reshape(f32[256,2,2048]{2,0,1:T(8,128)} %convolution_bitcast_fusion) | data formatting | bytes 8388608 | tf_op jit(solution)/shard_map/reshape | solution.py:79
  115.8 6.9 %copy.52 = f32[128,2,2,2048]{3,1,2,0:T(2,128)} copy(f32[128,2,2,2048]{3,1,0,2:T(2,128)} %reshape.67) | data formatting | bytes 8388608 | tf_op jit(solution)/shard_map/reshape | solution.py:79
  122.8 5.8 %all-to-all-start.2 = ((f32[128,2,2,2048]{3,2,1,0:T(2,128)}), f32[128,2,2,2048]{3,2,1,0:T(2,128)}, u32[]{:S(2)}, u32[]{:S(2)}) async-start(f32[128,2,2,2048]{3,2,1,0:T(2,128)} %bitcast.24), calls=%async_computation.2 | async-start | bytes 8388608 | tf_op jit(solution)/shard_map/all_to_all | solution.py:81
  128.6 0.1 copy.39
  128.7 0.1 copy.45
  128.8 0.1 reshape.89
  128.9 5.7 %convolution_convert_fusion.1 = bf16[2,512,2048]{2,1,0:T(8,128)(2,1)} fusion(bf16[2,256,2048]{2,1,0:T(8,128)(2,1)} %reshape.64, f32[2,256,1024]{2,1,0:T(8,128)} %copy-done.3), kind=kOutput, calls=%fused_computation.6 | convolution fusion | flops 1078460416 | bytes 8388608 | tf_op jit(solution)/shard_map/jrf,jrd->jfd/dot_general | solution.py:75
  134.6 2.4 %convolution_convert_fusion = bf16[2,2048,1024]{2,1,0:T(8,128)(2,1)S(1)} fusion(bf16[2,256,2048]{2,1,0:T(8,128)(2,1)S(1)} %reshape.66, bf16[2,256,512]{2,1,0:T(8,128)(2,1)S(1)} %get-tuple-element.9, bf16[2,256,512]{2,1,0:T(8,128)(2,1)S(1)} %get-tuple-element.8), kind=kOutput, calls=%fused_computation.3 | convolution fusion | flops 2153775104 | bytes 11534336 | tf_op jit(solution)/shard_map/jrd,jrf->jdf/dot_general | solution.py:72
  137.0 0.0 copy-start.1
  137.0 3.9 %fusion.15 = (bf16[2,2048,512]{2,1,0:T(8,128)(2,1)}, bf16[2,2048,512]{2,1,0:T(8,128)(2,1)}) fusion(bf16[2,2048,1024]{2,1,0:T(8,128)(2,1)S(1)} %convolution_convert_fusion), kind=kLoop, calls=%fused_computation.43 | loop fusion | bytes 16777216 | tf_op jit(solution)/shard_map/slice | solution.py:93
  140.8 39.9 %all-to-all-done.2 = f32[128,2,2,2048]{3,2,1,0:T(2,128)} async-done(((f32[128,2,2,2048]{3,2,1,0:T(2,128)}), f32[128,2,2,2048]{3,2,1,0:T(2,128)}, u32[]{:S(2)}, u32[]{:S(2)}) %all-to-all-start.2) | async-done | bytes 4194336 | tf_op jit(solution)/shard_map/all_to_all | solution.py:81
  180.8 3.9 %bitcast_reduce_fusion = f32[8,2,2,2048]{3,2,1,0:T(2,128)S(1)} fusion(f32[128,2,2,2048]{3,2,1,0:T(2,128)} %all-to-all-done.2), kind=kLoop, calls=%fused_computation.4 | loop fusion | flops 983040 | bytes 4456448 | tf_op jit(solution)/shard_map/reduce_sum | solution.py:84
  184.7 0.2 reshape.69
  184.9 0.7 gather_fusion.2
  185.6 0.1 reshape.88
  185.7 1.1 select_reduce_fusion
  (12 shorter events, 0.0 us)
Async XLA Ops:
  0.6 1.7 copy-start
  2.4 15.8 %copy-start.2 = (bf16[16,2048]{1,0:T(8,128)(2,1)S(1)}, bf16[16,2048]{1,0:T(8,128)(2,1)}, u32[]{:S(2)}) copy-start(bf16[16,2048]{1,0:T(8,128)(2,1)} %param.8) | copy-start | bytes 196612
  6.8 41.4 %all-to-all-start = ((bf16[128,2,2,2048]{3,2,1,0:T(2,128)(2,1)}), bf16[128,2,2,2048]{3,2,1,0:T(2,128)(2,1)S(1)}, u32[]{:S(2)}, u32[]{:S(2)}) async-start(bf16[128,2,2,2048]{3,2,1,0:T(2,128)(2,1)} %bitcast.26), calls=%async_computation | async-start | bytes 4194304 | tf_op jit(solution)/shard_map/all_to_all | solution.py:46
  51.6 35.6 %all-to-all-start.1 = ((bf16[128,2,2,2048]{3,2,1,0:T(2,128)(2,1)}), bf16[128,2,2,2048]{3,2,1,0:T(2,128)(2,1)}, u32[]{:S(2)}, u32[]{:S(2)}) async-start(bf16[128,2,2,2048]{3,2,1,0:T(2,128)(2,1)} %bitcast.27), calls=%async_computation.1 | async-start | bytes 4194304 | tf_op jit(solution)/shard_map/all_to_all | solution.py:39
  57.6 4.7 %copy-start.5 = (bf16[2,2048,512]{2,1,0:T(8,128)(2,1)S(1)}, bf16[2,2048,512]{2,1,0:T(8,128)(2,1)}, u32[]{:S(2)}) copy-start(bf16[2,2048,512]{2,1,0:T(8,128)(2,1)} %param.14) | copy-start | bytes 12582916
  94.3 5.9 %copy-start.4 = (bf16[2,256,2048]{2,1,0:T(8,128)(2,1)S(1)}, bf16[2,256,2048]{2,1,0:T(8,128)(2,1)}, u32[]{:S(2)}) copy-start(bf16[2,256,2048]{2,1,0:T(8,128)(2,1)} %reshape.64) | copy-start | bytes 6291460
  94.3 5.9 %copy-start.6 = (bf16[2,512,2048]{2,1,0:T(8,128)(2,1)S(1)}, bf16[2,512,2048]{2,1,0:T(8,128)(2,1)}, u32[]{:S(2)}) copy-start(bf16[2,512,2048]{2,1,0:T(8,128)(2,1)} %param.15) | copy-start | bytes 12582916
  100.2 2.0 %copy-start.3 = (f32[2,256,1024]{2,1,0:T(8,128)}, f32[2,256,1024]{2,1,0:T(8,128)S(1)}, u32[]{:S(2)}) copy-start(f32[2,256,1024]{2,1,0:T(8,128)S(1)} %fusion.16) | copy-start | bytes 6291460
  122.8 58.0 %all-to-all-start.2 = ((f32[128,2,2,2048]{3,2,1,0:T(2,128)}), f32[128,2,2,2048]{3,2,1,0:T(2,128)}, u32[]{:S(2)}, u32[]{:S(2)}) async-start(f32[128,2,2,2048]{3,2,1,0:T(2,128)} %bitcast.24), calls=%async_computation.2 | async-start | bytes 8388608 | tf_op jit(solution)/shard_map/all_to_all | solution.py:81
  137.0 49.8 %copy-start.1 = (bf16[16,2048]{1,0:T(8,128)(2,1)S(1)}, bf16[16,2048]{1,0:T(8,128)(2,1)}, u32[]{:S(2)}) copy-start(bf16[16,2048]{1,0:T(8,128)(2,1)} %param.9) | copy-start | bytes 196612
where the time goes:
time: 189 us; the launch traced here: 187 us
  waiting for transfers between devices  84.8 us (45%)
  local copies, waits for them, and re-layouts  47.5 us (25%)
  matrix products  23.7 us (13%)
  starting transfers between devices  22.9 us (12%)
  other arithmetic  7.02 us (4%)
    all_to_all x1, waiting for transfers between devices, per_device(): lax.all_to_all(partial_all, ('ex', 'ey', 'dp'), split_axis=0, concat_axis...  39.9 us
    all_to_all x1, waiting for transfers between devices, per_device(): lax.all_to_all(jnp.repeat(send_grad, shards, axis=0), ('ex', 'ey', 'dp'),...  29.1 us
    all_to_all x1, waiting for transfers between devices, per_device(): lax.all_to_all(jnp.repeat(send_input, shards, axis=0), ('ex', 'ey', 'dp')...  15.7 us
    reshape x2, local copies, waits for them, and re-layouts, per_device(): partial_all.reshape(ex_count * shards, capacity, local_count, model_width)  12.7 us
    all_to_all x1, starting transfers between devices, per_device(): lax.all_to_all(jnp.repeat(send_grad, shards, axis=0), ('ex', 'ey', 'dp'),...  11.1 us
    dot_general x1, matrix products, per_device(): jnp.einsum('jrf,jdf->rjd', grad_pair, weight_pair, preferred_element_type...  7.76 us
    all_to_all x1, starting transfers between devices, per_device(): lax.all_to_all(jnp.repeat(send_input, shards, axis=0), ('ex', 'ey', 'dp')...  5.96 us
    dot_general x1, matrix products, per_device(): jnp.einsum('jrd,jdf->jrf', rows_input, weight_pair, preferred_element_typ...  5.86 us
  transfers between devices with their start and end apart: 3, of which 3 were waited for; matrix products, arithmetic and copies ran while one was open for 15% of the time, Pallas kernels for 0%

commit v1 on v0

v1 whole, which is shorter than its diff:
```python
import jax
import jax.numpy as jnp
from jax import lax
from jax.experimental import pallas as pl
from jax.experimental.pallas import tpu as pltpu
from jax.sharding import PartitionSpec as P

MESH = pl.DeviceIdType.MESH
F32 = jnp.float32
BF16 = jnp.bfloat16

NX = 4
NZ = 4
PEERS = 8
BLOCKS = 16
TILE = 16


def dot(a, b, ca, cb):
    return lax.dot_general(a, b, (((ca,), (cb,)), ((), ())), preferred_element_type=F32)


def onehot(mask):
    return jnp.where(mask, 1.0, 0.0).astype(BF16)


def block_row(dc, dyl, dz):
    return TILE * (dc * 8 + dyl * 4 + dz)


def main_kernel(
    tok_ref, cot_ref, rw_ref, ids_ref, slots_ref, wg_hbm, wu_hbm, wd_hbm,
    gtok_ref, rows, hid_ref, gg_ref, gu_ref,
    wg, wu, wd, send1, recv1, acc, pair_out, pair_in,
    z2_out, z2_in, zp_out, zp_in, zm_out, zm_in, y0_out, y0_in, y1_out, y1_in,
    ret_out, ret_in, w_sem, send_sem, recv_sem,
):
    ex, ey, dp = lax.axis_index("ex"), lax.axis_index("ey"), lax.axis_index("dp")
    yh, x = ex // NX, ex % NX
    yl, core = ey // 2, ey % 2
    width = tok_ref.shape[1]
    half, quarter = width // 2, width // 4
    hidden = wg.shape[2]

    def peer(k, sign):
        dyh, dx = k // NX, k % NX
        other_yl = (yl + dyh) % 2
        return (((yh + dyh) % 2) * NX + (x + sign * dx + NX) % NX, other_yl * 2 + core, dp)

    z_plus = (ex, ey, (dp + 1) % NZ)
    z_minus = (ex, ey, (dp + NZ - 1) % NZ)
    y_pair = (ex, (1 - yl) * 2 + core, dp)
    sibling = (ex, yl * 2 + (1 - core), dp)

    barrier = pltpu.get_barrier_semaphore()
    partners = [peer(k, 1) for k in range(1, PEERS)] + [z_plus, z_minus, y_pair, sibling]
    for device in partners:
        pl.semaphore_signal(barrier, inc=1, device_id=device, device_id_type=MESH)

    loads = []
    for e in range(2):
        for n, (source, target) in enumerate(((wg_hbm, wg), (wu_hbm, wu), (wd_hbm, wd))):
            copy = pltpu.make_async_copy(source.at[e], target.at[e], w_sem.at[e * 3 + n])
            copy.start()
            loads.append(copy)

    lane = lax.broadcasted_iota(jnp.int32, (16, 128), 1)
    piece = lane // 16
    group = ((yh + piece // NX) % 2) * NX + (x + piece % NX) % NX
    slot_of = lane % 2
    expert_of = group * 2 + (lane // 2) % 2
    ids, slots = ids_ref[...], slots_ref[...]
    match = [
        jnp.where((ids[:, k : k + 1] == expert_of) & (slots[:, k : k + 1] == slot_of), 1.0, 0.0)
        for k in range(2)
    ]
    rw = rw_ref[...]
    cot = cot_ref[...].astype(F32)
    routed = [(rw[:, k : k + 1] * cot).astype(BF16) for k in range(2)]
    stacked = jnp.concatenate([tok_ref[...], routed[0], routed[1]], axis=0)
    is_grad = (lane // 4) % 2 == 1
    pick = jnp.concatenate(
        [
            jnp.where(is_grad, 0.0, match[0] + match[1]),
            jnp.where(is_grad, match[0], 0.0),
            jnp.where(is_grad, match[1], 0.0),
        ],
        axis=0,
    )
    lane48 = lax.broadcasted_iota(jnp.int32, (48, 128), 1)
    upper = (lane48 // 8) % 2 == 1
    built = dot(jnp.where(upper, 0.0, pick).astype(BF16), stacked[:, :half], 0, 0)
    built += dot(jnp.where(upper, pick, 0.0).astype(BF16), stacked[:, half:], 0, 0)
    send1[...] = built.astype(BF16)

    pl.semaphore_wait(barrier, len(partners))

    count = [0, 0]
    sent = []

    def remote(src, dst, device, recv_index):
        index = count[0]
        count[0] += 1
        copy = pltpu.make_async_remote_copy(
            src_ref=src,
            dst_ref=dst,
            send_sem=send_sem.at[index],
            recv_sem=recv_sem.at[recv_index],
            device_id=device,
            device_id_type=MESH,
        )
        copy.start()
        sent.append(copy)
        return copy

    def fresh():
        count[1] += 1
        return count[1] - 1

    first = []
    for k in range(1, PEERS):
        part = pl.ds(k * TILE, TILE)
        first.append(remote(send1.at[part], recv1.at[part], peer(k, 1), fresh()))
    recv1[0:TILE] = send1[0:TILE]
    for copy in first:
        copy.wait_recv()
    row_o = lax.broadcasted_iota(jnp.int32, (64, 128), 0)
    lane_o = lax.broadcasted_iota(jnp.int32, (64, 128), 1)
    wanted = (
        ((row_o % 16) // 2) * 16 + ((row_o // 16) % 2) * 4 + (row_o // 32) * 2 + row_o % 2
    )
    pieces = recv1[...]
    for h in range(2):
        block = dot(onehot(lane_o == wanted + 8 * h), pieces, 1, 0).astype(BF16)
        for s in range(4):
            rows[s, 0:TILE, h * half : (h + 1) * half] = block[s * TILE : (s + 1) * TILE]

    arrive = {}

    def move(s, here, there, device):
        src = rows.at[s, pl.ds(block_row(*here), TILE)]
        dst = rows.at[s, pl.ds(block_row(*there), TILE)]
        arrive[s, there] = remote(src, dst, device, fresh())

    def arrived(s, block):
        arrive[s, block].wait_recv()

    def share(s, dyl):
        src = rows.at[s, pl.ds(block_row(0, dyl, 0), 4 * TILE)]
        dst = rows.at[s, pl.ds(block_row(1, dyl, 0), 4 * TILE)]
        arrive[s, "share", dyl] = remote(src, dst, sibling, fresh())

    def ring(s, dyl):
        move(s, (0, dyl, 0), (0, dyl, 3), z_plus)
        move(s, (0, dyl, 0), (0, dyl, 1), z_minus)

    def onward(s, dyl, up):
        if up:
            move(s, (0, dyl, 3), (0, dyl, 2), z_plus)
        else:
            move(s, (0, dyl, 1), (0, dyl, 2), z_minus)

    for e in range(2):
        xs, gs = 2 * e, 2 * e + 1
        move(xs, (0, 0, 0), (0, 1, 0), y_pair)
        ring(gs, 0)
        ring(xs, 0)
        move(gs, (0, 0, 0), (0, 1, 0), y_pair)
    for e in range(2):
        xs, gs = 2 * e, 2 * e + 1
        up = e == 0
        arrived(xs, (0, 1, 0))
        ring(xs, 1)
        arrived(gs, (0, 0, 3))
        arrived(gs, (0, 0, 1))
        onward(gs, 0, not up)
        move(gs, (0, 0, 3), (0, 1, 3), y_pair)
        move(gs, (0, 0, 1), (0, 1, 1), y_pair)
        arrived(xs, (0, 0, 3))
        arrived(xs, (0, 0, 1))
        onward(xs, 0, up)
    for e in range(2):
        xs, gs = 2 * e, 2 * e + 1
        up = e == 0
        arrived(xs, (0, 1, 3))
        arrived(xs, (0, 1, 1))
        onward(xs, 1, up)
        arrived(gs, (0, 0, 2))
        move(gs, (0, 0, 2), (0, 1, 2), y_pair)
        share(gs, 0)
        arrived(xs, (0, 0, 2))
        share(xs, 0)
    for e in range(2):
        xs, gs = 2 * e, 2 * e + 1
        arrived(xs, (0, 1, 2))
        share(xs, 1)
        for dz in range(4):
            arrived(gs, (0, 1, dz))
        share(gs, 1)

    c0, c1 = 0.7978845608028654, 0.044715
    pair = []
    for e in range(2):
        xs, gs = 2 * e, 2 * e + 1
        for s in (xs, gs):
            for dyl in range(2):
                arrive[s, "share", dyl].wait_recv()
        for n in range(3):
            loads[e * 3 + n].wait()
        step = hidden // 2
        for f in range(2):
            cols = pl.ds(f * step, step)
            pre_gate = dot(rows[xs], wg[e, :, cols], 1, 0)
            pre_up = dot(rows[xs], wu[e, :, cols], 1, 0)
            grad_hidden = dot(rows[gs], wd[e, cols, :], 1, 1)
            square = pre_gate * pre_gate
            t = jnp.tanh(c0 * (pre_gate + c1 * (pre_gate * square)))
            cdf = 0.5 * (1.0 + t)
            act = pre_gate * cdf
            slope = cdf + (0.5 * c0) * pre_gate * (1.0 - t * t) * (1.0 + (3.0 * c1) * square)
            hid_ref[e, :, cols] = (act * pre_up).astype(BF16)
            gu_ref[e, :, cols] = (grad_hidden * act).astype(BF16)
            gg_ref[e, :, cols] = (grad_hidden * pre_up * slope).astype(BF16)
        step = width // 4
        for d in range(4):
            cols = pl.ds(d * step, step)
            part = dot(gg_ref[e], wg[e, cols, :], 1, 1) + dot(gu_ref[e], wu[e, cols, :], 1, 1)
            acc[e, :, cols] = part[: 8 * TILE]
            pair_out[e, :, cols] = part[8 * TILE :].astype(BF16)
        pair.append(remote(pair_out.at[e], pair_in.at[e], sibling, fresh()))

    pair[0].wait_recv()
    acc[0] += pair_in[0].astype(F32)
    z2_out[0] = acc[0, 2 * TILE : 3 * TILE].astype(BF16)
    z2_out[1] = acc[0, 6 * TILE : 7 * TILE].astype(BF16)
    z2 = [
        remote(z2_out.at[0], z2_in.at[0], z_plus, fresh()),
        remote(z2_out.at[1], z2_in.at[1], z_minus, fresh()),
    ]
    zp_out[1] = acc[0, 5 * TILE : 6 * TILE].astype(BF16)
    zm_out[0] = acc[0, 3 * TILE : 4 * TILE].astype(BF16)
    zp = {1: remote(zp_out.at[1], zp_in.at[1], z_plus, fresh())}
    zm = {0: remote(zm_out.at[0], zm_in.at[0], z_minus, fresh())}

    pair[1].wait_recv()
    acc[1] += pair_in[1].astype(F32)
    y1_out[...] = acc[1, 4 * TILE : 8 * TILE].astype(BF16)
    y1 = remote(y1_out, y1_in, y_pair, fresh())

    z2[0].wait_recv()
    zp_out[0] = (acc[0, TILE : 2 * TILE] + z2_in[0].astype(F32)).astype(BF16)
    zp[0] = remote(zp_out.at[0], zp_in.at[0], z_plus, fresh())
    z2[1].wait_recv()
    zm_out[1] = (acc[0, 7 * TILE : 8 * TILE] + z2_in[1].astype(F32)).astype(BF16)
    zm[1] = remote(zm_out.at[1], zm_in.at[1], z_minus, fresh())

    y1.wait_recv()
    acc[1, 0 : 4 * TILE] += y1_in[...].astype(F32)
    z2_out[2] = acc[1, 2 * TILE : 3 * TILE].astype(BF16)
    z3 = [
        remote(z2_out.at[2, :, pl.ds(0, half)], z2_in.at[2, :, pl.ds(0, half)], z_plus, fresh()),
        remote(z2_out.at[2, :, pl.ds(half, half)], z2_in.at[2, :, pl.ds(half, half)], z_minus, fresh()),
    ]

    zp[1].wait_recv()
    zm[1].wait_recv()
    y0_out[...] = (
        acc[0, 4 * TILE : 5 * TILE] + zp_in[1].astype(F32) + zm_in[1].astype(F32)
    ).astype(BF16)
    y0 = remote(y0_out, y0_in, y_pair, fresh())

    z3[0].wait_recv()
    z3[1].wait_recv()
    zp_out[2, :, 0:half] = (
        acc[1, TILE : 2 * TILE, 0:half] + z2_in[2, :, 0:half].astype(F32)
    ).astype(BF16)
    zp_out[2, :, half:] = acc[1, TILE : 2 * TILE, half:].astype(BF16)
    zm_out[2, :, half:] = (
        acc[1, 3 * TILE : 4 * TILE, half:] + z2_in[2, :, half:].astype(F32)
    ).astype(BF16)
    zm_out[2, :, 0:half] = acc[1, 3 * TILE : 4 * TILE, 0:half].astype(BF16)
    zp[2] = remote(zp_out.at[2], zp_in.at[2], z_plus, fresh())
    zm[2] = remote(zm_out.at[2], zm_in.at[2], z_minus, fresh())

    zp[0].wait_recv()
    zm[0].wait_recv()
    y0.wait_recv()
    total0 = (
        acc[0, 0:TILE] + zp_in[0].astype(F32) + zm_in[0].astype(F32) + y0_in[...].astype(F32)
    )
    zp[2].wait_recv()
    zm[2].wait_recv()
    total1 = acc[1, 0:TILE] + zp_in[2].astype(F32) + zm_in[2].astype(F32)
    totals = jnp.concatenate([total0.astype(BF16), total1.astype(BF16)], axis=0)

    row_r = lax.broadcasted_iota(jnp.int32, (128, 32), 0)
    lane_r = lax.broadcasted_iota(jnp.int32, (128, 32), 1)
    from_row = ((row_r // 2) % 2) * 16 + (row_r // 16) * 2 + row_r % 2
    outgoing = None
    for q in range(4):
        choose = onehot((lane_r == from_row) & ((row_r // 4) % 4 == q))
        term = dot(choose, totals[:, q * quarter : (q + 1) * quarter], 1, 0)
        outgoing = term if outgoing is None else outgoing + term
    ret_out[...] = outgoing.astype(BF16)
    last = []
    for k in range(1, PEERS):
        part = pl.ds(k * TILE, TILE)
        last.append(remote(ret_out.at[part], ret_in.at[part], peer(k, -1), fresh()))
    ret_in[0:TILE] = ret_out[0:TILE]
    for copy in last:
        copy.wait_recv()
    both = match[0] + match[1]
    for q in range(4):
        choose = jnp.where((lane // 4) % 4 == q, both, 0.0).astype(BF16)
        gtok_ref[:, q * quarter : (q + 1) * quarter] = dot(choose, ret_in[...], 1, 0).astype(BF16)
    for copy in sent:
        copy.wait_send()


def weight_kernel(x_ref, g_ref, hid_ref, gg_ref, gu_ref, dgate_ref, dup_ref, ddown_ref):
    dgate_ref[0] = dot(x_ref[0], gg_ref[0], 0, 0).astype(BF16)
    dup_ref[0] = dot(x_ref[0], gu_ref[0], 0, 0).astype(BF16)
    ddown_ref[0] = dot(hid_ref[0], g_ref[0], 0, 0).astype(BF16)


def per_device(tokens, cotangent, route_weights, expert_ids, slot_ids, gate, up, down):
    local, width, hidden = gate.shape
    count = tokens.shape[0]
    total = BLOCKS * TILE
    vmem = pl.BlockSpec(memory_space=pltpu.VMEM)
    anywhere = pl.BlockSpec(memory_space=pl.ANY)
    grads, rows, hid, gg, gu = pl.pallas_call(
        main_kernel,
        out_shape=(
            jax.ShapeDtypeStruct((count, width), BF16),
            jax.ShapeDtypeStruct((4, total, width), BF16),
            jax.ShapeDtypeStruct((local, total, hidden), BF16),
            jax.ShapeDtypeStruct((local, total, hidden), BF16),
            jax.ShapeDtypeStruct((local, total, hidden), BF16),
        ),
        in_specs=[vmem] * 5 + [anywhere] * 3,
        out_specs=[vmem] * 5,
        scratch_shapes=[
            pltpu.VMEM((local, width, hidden), BF16),
            pltpu.VMEM((local, width, hidden), BF16),
            pltpu.VMEM((local, hidden, width), BF16),
            pltpu.VMEM((128, width // 2), BF16),
            pltpu.VMEM((128, width // 2), BF16),
            pltpu.VMEM((2, total // 2, width), F32),
            pltpu.VMEM((2, total // 2, width), BF16),
            pltpu.VMEM((2, total // 2, width), BF16),
            pltpu.VMEM((3, TILE, width), BF16),
            pltpu.VMEM((3, TILE, width), BF16),
            pltpu.VMEM((3, TILE, width), BF16),
            pltpu.VMEM((3, TILE, width), BF16),
            pltpu.VMEM((3, TILE, width), BF16),
            pltpu.VMEM((3, TILE, width), BF16),
            pltpu.VMEM((TILE, width), BF16),
            pltpu.VMEM((TILE, width), BF16),
            pltpu.VMEM((4 * TILE, width), BF16),
            pltpu.VMEM((4 * TILE, width), BF16),
            pltpu.VMEM((128, width // 4), BF16),
            pltpu.VMEM((128, width // 4), BF16),
            pltpu.SemaphoreType.DMA((6,)),
            pltpu.SemaphoreType.DMA((80,)),
            pltpu.SemaphoreType.DMA((80,)),
        ],
        compiler_params=pltpu.CompilerParams(
            collective_id=0, has_side_effects=True, vmem_limit_bytes=56 * 1024 * 1024
        ),
    )(tokens, cotangent, route_weights, expert_ids, slot_ids, gate, up, down)

    parts = 4
    step = width // parts
    row_block = (1, total, step)
    hid_spec = pl.BlockSpec((1, total, hidden), lambda e, d: (e, 0, 0))
    tall = pl.BlockSpec((1, step, hidden), lambda e, d: (e, d, 0))
    wide = pl.BlockSpec((1, hidden, step), lambda e, d: (e, 0, d))
    dgate, dup, ddown = pl.pallas_call(
        weight_kernel,
        grid=(local, parts),
        out_shape=(
            jax.ShapeDtypeStruct((local, width, hidden), BF16),
            jax.ShapeDtypeStruct((local, width, hidden), BF16),
            jax.ShapeDtypeStruct((local, hidden, width), BF16),
        ),
        in_specs=[
            pl.BlockSpec(row_block, lambda e, d: (2 * e, 0, d)),
            pl.BlockSpec(row_block, lambda e, d: (2 * e + 1, 0, d)),
            hid_spec,
            hid_spec,
            hid_spec,
        ],
        out_specs=[tall, tall, wide],
        compiler_params=pltpu.CompilerParams(vmem_limit_bytes=32 * 1024 * 1024),
    )(rows, rows, hid, gg, gu)
    return (grads, dgate, dup, ddown)


def solution(mesh):
    return jax.shard_map(
        per_device,
        mesh=mesh,
        in_specs=(
            P(("ex", "ey", "dp"), None),
            P(("ex", "ey", "dp"), None),
            P(("ex", "ey", "dp"), None),
            P(("ex", "ey", "dp"), None),
            P(("ex", "ey", "dp"), None),
            P("ex", None, ("ey", "dp")),
            P("ex", None, ("ey", "dp")),
            P("ex", ("ey", "dp"), None),
        ),
        out_specs=(
            P(("ex", "ey", "dp"), None),
            P("ex", None, ("ey", "dp")),
            P("ex", None, ("ey", "dp")),
            P("ex", ("ey", "dp"), None),
        ),
        check_vma=False,
    )
```

time: 189 us -> 80.8 us (0.43)
  waiting for transfers between devices: 84.8 us -> 0 us
  Pallas kernels: 0 us -> 69.8 us
  local copies, waits for them, and re-layouts: 47.5 us -> 9.99 us
  matrix products: 23.7 us -> 0 us
  starting transfers between devices: 22.9 us -> 0 us
  other arithmetic: 7.02 us -> 0 us
    all_to_all x3 -> x0, waiting for transfers between devices: 84.8 us -> none  [the longest x1 39.9 us: per_device(): lax.all_to_all(partial_all, ('ex', 'ey', 'dp'), split_axis=0, concat_axis...]
    pallas_call x0 -> x2, Pallas kernels: none -> 69.8 us  [the longest x1 62.5 us: per_device(): pl.pallas_call(main_kernel, out_shape=(jax.ShapeDtypeStruct((count, width...]
    dot_general x5 -> x0, matrix products: 23.7 us -> none  [the longest x1 7.76 us: per_device(): jnp.einsum('jrf,jdf->rjd', grad_pair, weight_pair, preferred_element_type...]
    all_to_all x3 -> x0, starting transfers between devices: 22.9 us -> none  [the longest x1 11.1 us: per_device(): lax.all_to_all(jnp.repeat(send_grad, shards, axis=0), ('ex', 'ey', 'dp'),...]
    reshape x5 -> x0, local copies, waits for them, and re-layouts: 19.8 us -> none  [the longest x2 12.7 us: per_device(): partial_all.reshape(ex_count * shards, capacity, local_count, model_width)]
    transpose x2 -> x0, local copies, waits for them, and re-layouts: 7.11 us -> none  [the longest x1 4.35 us: per_device(): jnp.transpose(rows_input, (1, 0, 2, 3))]
    broadcast_in_dim x4 -> x0, local copies, waits for them, and re-layouts: 7 us -> none  [the longest x1 3.41 us: per_device(): jnp.repeat(send_grad, shards, axis=0)]
    reduce_sum x4 -> x0, other arithmetic: 5.83 us -> none  [the longest x1 3.92 us: per_device(): jnp.sum(arrived.reshape(ex_count, shards, local_count, capacity, model_wi...]
  transfers between devices with their start and end apart: 3 -> 0, of which waited for: 3 -> 0; matrix products, arithmetic and copies ran while one was open for 15% -> 0% of each run, Pallas kernels for 0% -> 0%
where the time goes in v1:
time: 80.8 us; the launch traced here: 80.4 us
  Pallas kernels  69.8 us (86%)
  local copies, waits for them, and re-layouts  9.99 us (12%)
    pallas_call x1, Pallas kernels, per_device(): pl.pallas_call(main_kernel, out_shape=(jax.ShapeDtypeStruct((count, width...  62.5 us
    unnamed x14, local copies, waits for them, and re-layouts  9.99 us
    pallas_call x1, Pallas kernels, per_device(): pl.pallas_call(weight_kernel, grid=(local, parts), out_shape=(jax.ShapeDt...  7.21 us

profile of v1, /device:TPU:0, one launch (start us, length us, event | category | flops | bytes accessed | tf_op | source)
XLA Modules:
  0.0 80.4 jit_solution(10416519780669470564)
XLA Ops:
  0.6 1.4 %copy.12.rw_ref = f32[16,2]{1,0:T(8,128)} copy(f32[16,2]{0,1:T(2,128)} %param.10) | data formatting | bytes 256 | tf_op args[2]
  2.0 1.4 %copy.13.ids_ref = s32[16,2]{1,0:T(8,128)} copy(s32[16,2]{0,1:T(2,128)} %param.11) | data formatting | bytes 256 | tf_op args[3]
  3.3 1.4 %copy.14.slots_ref = s32[16,2]{1,0:T(8,128)} copy(s32[16,2]{0,1:T(2,128)} %param.12) | data formatting | bytes 256 | tf_op args[4]
  4.7 62.5 %shard_map.111 = (bf16[16,2048]{1,0:T(8,128)(2,1)}, bf16[4,256,2048]{2,1,0:T(8,128)(2,1)}, bf16[2,256,512]{2,1,0:T(8,128)(2,1)}, bf16[2,256,512]{2,1,0:T(8,128)(2,1)}, bf16[2,256,512]{2,1,0:T(8,128)(2,1)}) custom-call(bf16[16,2048]{1,0:T(8,128)(2,1)} %tok_ref.1, bf16[16,2048]{1,0:T(8,128)(2,1)} %cot_ref.1, f32[16,2]{1,0:T(8,128)} %copy.12.rw_ref, ...), custom_call_target="tpu_custom_call" | custom-call | tf_op jit(solution)/shard_map/pallas_call | solution.py:332
  67.2 0.0 copy-start
  67.3 2.2 %copy-done = bf16[4,256,2048]{2,1,0:T(8,128)(2,1)S(1)} copy-done((bf16[4,256,2048]{2,1,0:T(8,128)(2,1)S(1)}, bf16[4,256,2048]{2,1,0:T(8,128)(2,1)}, u32[]{:S(2)}) %copy-start) | copy-done | bytes 4194328
  69.4 0.0 copy-start.1
  69.4 1.0 %copy-done.1 = bf16[2,256,512]{2,1,0:T(8,128)(2,1)S(1)} copy-done((bf16[2,256,512]{2,1,0:T(8,128)(2,1)S(1)}, bf16[2,256,512]{2,1,0:T(8,128)(2,1)}, u32[]{:S(2)}) %copy-start.1) | copy-done | bytes 524312
  70.5 0.0 copy-start.2
  70.5 1.0 %copy-done.2 = bf16[2,256,512]{2,1,0:T(8,128)(2,1)S(1)} copy-done((bf16[2,256,512]{2,1,0:T(8,128)(2,1)S(1)}, bf16[2,256,512]{2,1,0:T(8,128)(2,1)}, u32[]{:S(2)}) %copy-start.2) | copy-done | bytes 524312
  71.5 0.0 copy-start.3
  71.5 1.0 %copy-done.3 = bf16[2,256,512]{2,1,0:T(8,128)(2,1)S(1)} copy-done((bf16[2,256,512]{2,1,0:T(8,128)(2,1)S(1)}, bf16[2,256,512]{2,1,0:T(8,128)(2,1)}, u32[]{:S(2)}) %copy-start.3) | copy-done | bytes 524312
  72.6 0.0 copy-start.4
  72.6 7.2 %shard_map.112 = (bf16[2,2048,512]{2,1,0:T(8,128)(2,1)}, bf16[2,2048,512]{2,1,0:T(8,128)(2,1)}, bf16[2,512,2048]{2,1,0:T(8,128)(2,1)}) custom-call(bf16[4,256,2048]{2,1,0:T(8,128)(2,1)S(1)} %copy-done, bf16[4,256,2048]{2,1,0:T(8,128)(2,1)S(1)} %copy-done, bf16[2,256,512]{2,1,0:T(8,128)(2,1)S(1)} %copy-done.1, bf16[2,256,512]{2,1,0:T(8,128)(2,1)S(1)} %copy-done.2, ...), custom_call_target="tpu_custom_call" | custom-call | tf_op jit(solution)/shard_map/pallas_call | solution.py:379
  79.8 0.0 copy-done.4
  79.8 0.6 copy.16
Async XLA Ops:
  67.2 2.2 %copy-start = (bf16[4,256,2048]{2,1,0:T(8,128)(2,1)S(1)}, bf16[4,256,2048]{2,1,0:T(8,128)(2,1)}, u32[]{:S(2)}) copy-start(bf16[4,256,2048]{2,1,0:T(8,128)(2,1)} %get-tuple-element.13.x_ref.g_ref) | copy-start | bytes 12582916
  69.4 1.0 %copy-start.1 = (bf16[2,256,512]{2,1,0:T(8,128)(2,1)S(1)}, bf16[2,256,512]{2,1,0:T(8,128)(2,1)}, u32[]{:S(2)}) copy-start(bf16[2,256,512]{2,1,0:T(8,128)(2,1)} %get-tuple-element.14.hid_ref) | copy-start | bytes 1572868
  70.5 1.0 %copy-start.2 = (bf16[2,256,512]{2,1,0:T(8,128)(2,1)S(1)}, bf16[2,256,512]{2,1,0:T(8,128)(2,1)}, u32[]{:S(2)}) copy-start(bf16[2,256,512]{2,1,0:T(8,128)(2,1)} %get-tuple-element.15.gg_ref) | copy-start | bytes 1572868
  71.5 1.0 %copy-start.3 = (bf16[2,256,512]{2,1,0:T(8,128)(2,1)S(1)}, bf16[2,256,512]{2,1,0:T(8,128)(2,1)}, u32[]{:S(2)}) copy-start(bf16[2,256,512]{2,1,0:T(8,128)(2,1)} %get-tuple-element.16.gu_ref) | copy-start | bytes 1572868
  72.6 7.2 %copy-start.4 = (bf16[16,2048]{1,0:T(8,128)(2,1)S(1)}, bf16[16,2048]{1,0:T(8,128)(2,1)}, u32[]{:S(2)}) copy-start(bf16[16,2048]{1,0:T(8,128)(2,1)} %get-tuple-element.24) | copy-start | bytes 196612

commit v2 on v0

v2 whole, which is shorter than its diff:
```python
import jax
import jax.numpy as jnp
from jax import lax
from jax.experimental import pallas as pl
from jax.experimental.pallas import tpu as pltpu
from jax.sharding import PartitionSpec as P

MESH = pl.DeviceIdType.MESH
F32 = jnp.float32
BF16 = jnp.bfloat16

NX = 4
NZ = 4
PEERS = 8
BLOCKS = 16
TILE = 16
HALF_ROWS = 8 * TILE


def dot(a, b, ca, cb):
    return lax.dot_general(a, b, (((ca,), (cb,)), ((), ())), preferred_element_type=F32)


def onehot(mask):
    return jnp.where(mask, 1.0, 0.0).astype(BF16)


def iota(shape, dim):
    return lax.broadcasted_iota(jnp.int32, shape, dim)


def block_row(dc, dyl, dz):
    return TILE * (dc * 8 + dyl * 4 + dz)


def main_kernel(
    tok_hbm, cot_hbm, rw_ref, ids_ref, slots_ref, wg_hbm, wu_hbm, wd_hbm,
    gtok_ref, dgate_ref, dup_ref, ddown_ref,
    tok_cot, rows, hid, gg, gu, pre, wg, wu, wd, send1, recv1, acc, pair_out, pair_in,
    back_out, back_in,
    ret_out, ret_in, load_sem, send_sem, recv_sem,
):
    ex, ey, dp = lax.axis_index("ex"), lax.axis_index("ey"), lax.axis_index("dp")
    yh, x = ex // NX, ex % NX
    yl, core = ey // 2, ey % 2
    width = rows.shape[2]
    half, quarter, eighth = width // 2, width // 4, width // 8
    hidden = wg.shape[2]

    def peer(k, sign):
        dyh, dx = k // NX, k % NX
        other_yl = (yl + dyh) % 2
        return (((yh + dyh) % 2) * NX + (x + sign * dx + NX) % NX, other_yl * 2 + core, dp)

    def mate(b):
        dyl, dz = b // NZ, b % NZ
        return (ex, (yl + dyl) % 2 * 2 + core, (dp + dz) % NZ)

    z_plus = (ex, ey, (dp + 1) % NZ)
    z_minus = (ex, ey, (dp + NZ - 1) % NZ)
    z_far = (ex, ey, (dp + 2) % NZ)
    y_pair = (ex, (1 - yl) * 2 + core, dp)
    sibling = (ex, yl * 2 + (1 - core), dp)

    barrier = pltpu.get_barrier_semaphore()
    partners = [peer(k, 1) for k in range(1, PEERS)] + [mate(b) for b in range(1, 8)] + [sibling]
    for device in partners:
        pl.semaphore_signal(barrier, inc=1, device_id=device, device_id_type=MESH)

    def load(src, dst, index):
        copy = pltpu.make_async_copy(src, dst, load_sem.at[index])
        copy.start()
        return copy

    tok_load = load(tok_hbm, tok_cot.at[0:16], 6)
    cot_load = load(cot_hbm, tok_cot.at[16:32], 7)
    weights = [
        load(src.at[e], dst.at[e], e * 3 + n)
        for e in range(2)
        for n, (src, dst) in enumerate(((wg_hbm, wg), (wu_hbm, wu), (wd_hbm, wd)))
    ]

    count = [0, 0]
    sent = []

    def remote(src, dst, device):
        copy = pltpu.make_async_remote_copy(
            src_ref=src,
            dst_ref=dst,
            send_sem=send_sem.at[count[0]],
            recv_sem=recv_sem.at[count[0]],
            device_id=device,
            device_id_type=MESH,
        )
        count[0] += 1
        copy.start()
        sent.append(copy)
        return copy

    ids, slots, rw = ids_ref[...], slots_ref[...], rw_ref[...]
    row = iota((128, 16), 0)
    piece = row // 16
    group = ((yh + piece // NX) % 2) * NX + (x + piece % NX) % NX

    def matches(e):
        expert, slot = group * 2 + e, row % 2
        return [
            jnp.where((ids[k : k + 1] == expert) & (slots[k : k + 1] == slot), 1.0, 0.0)
            for k in range(2)
        ]

    def build(e):
        m = matches(e)
        is_grad = (row // 2) % 2 == 1
        any_match = m[0] + m[1]
        scale = jnp.sum(m[0] * rw[0:1] + m[1] * rw[1:2], axis=1, keepdims=True)
        scale = jnp.where(is_grad[:, 0:1], scale, 1.0)
        pick = jnp.concatenate(
            [jnp.where(is_grad, 0.0, any_match), jnp.where(is_grad, any_match, 0.0)], axis=1
        )
        part_of = (iota((128, 32), 0) // 4) % 4
        total = None
        for q in range(4):
            choose = jnp.where(part_of == q, pick, 0.0).astype(BF16)
            term = dot(choose, tok_cot[:, q * quarter : (q + 1) * quarter], 1, 0)
            total = term if total is None else total + term
        send1[e] = (total * scale).astype(BF16)

    first = {}

    def over_ex(e):
        first[e] = []
        for k in range(1, PEERS):
            part = pl.ds(k * TILE, TILE)
            first[e].append(remote(send1.at[e, part], recv1.at[e, part], peer(k, 1)))
        recv1[e, 0:TILE] = send1[e, 0:TILE]

    def form(e):
        for copy in first[e]:
            copy.wait_recv()
        out, lane = iota((32, 128), 0), iota((32, 128), 1)
        source = ((out % 16) // 2) * 16 + (out // 16) * 2 + out % 2
        for q in range(4):
            block = dot(onehot(lane == source + 4 * q), recv1[e], 1, 0).astype(BF16)
            cols = slice(q * quarter, (q + 1) * quarter)
            rows[2 * e, 0:TILE, cols] = block[0:TILE]
            rows[2 * e + 1, 0:TILE, cols] = block[TILE:]

    arrive = {}

    def move(s, here, there, device):
        src = rows.at[s, pl.ds(block_row(*here), TILE)]
        dst = rows.at[s, pl.ds(block_row(*there), TILE)]
        arrive[s, there] = remote(src, dst, device)

    def share(s, dyl, dz):
        move(s, (0, dyl, dz), (1, dyl, dz), sibling)

    def arrived(s, *block):
        arrive[s, block].wait_recv()

    def around(s, dyl):
        move(s, (0, dyl, 0), (0, dyl, 3), z_plus)
        move(s, (0, dyl, 0), (0, dyl, 1), z_minus)
        move(s, (0, dyl, 0), (0, dyl, 2), z_far)

    def across(s, dz):
        move(s, (0, 0, dz), (0, 1, dz), y_pair)

    def pass_on(s, dyl, dz):
        arrived(s, 0, dyl, dz)
        share(s, dyl, dz)

    def pass_across(s, dz):
        arrived(s, 0, 0, dz)
        across(s, dz)
        share(s, 0, dz)

    def shared(s):
        for dyl in range(2):
            for dz in range(4):
                arrived(s, 1, dyl, dz)

    c0, c1 = 0.7978845608028654, 0.044715
    step = hidden // 2

    def forward_inputs(e, f):
        cols = pl.ds(f * step, step)
        pre[0, :, cols] = dot(rows[2 * e], wg[e, :, cols], 1, 0)
        pre[1, :, cols] = dot(rows[2 * e], wu[e, :, cols], 1, 0)

    def forward_grads(e, f):
        cols = pl.ds(f * step, step)
        grad_hidden = dot(rows[2 * e + 1], wd[e, cols, :], 1, 1)
        pre_gate, pre_up = pre[0, :, cols], pre[1, :, cols]
        square = pre_gate * pre_gate
        t = jnp.tanh(c0 * (pre_gate + c1 * (pre_gate * square)))
        cdf = 0.5 * (1.0 + t)
        act = pre_gate * cdf
        slope = cdf + (0.5 * c0) * pre_gate * (1.0 - t * t) * (1.0 + (3.0 * c1) * square)
        hid[e, :, cols] = (act * pre_up).astype(BF16)
        gu[e, :, cols] = (grad_hidden * act).astype(BF16)
        gg[e, :, cols] = (grad_hidden * pre_up * slope).astype(BF16)

    pair = {}

    def input_grad(e, d):
        cols = pl.ds(d * quarter, quarter)
        part = dot(gg[e], wg[e, cols, :], 1, 1) + dot(gu[e], wu[e, cols, :], 1, 1)
        pair_out[e, :, cols] = part[HALF_ROWS:].astype(BF16)
        acc[e, :, cols] = part[:HALF_ROWS]
        pair[e, d] = remote(pair_out.at[e, :, cols], pair_in.at[e, :, cols], sibling)

    def weight_grad(e, which):
        if which == 0:
            dgate_ref[e] = dot(rows[2 * e], gg[e], 0, 0).astype(BF16)
        elif which == 1:
            dup_ref[e] = dot(rows[2 * e], gu[e], 0, 0).astype(BF16)
        else:
            ddown_ref[e] = dot(hid[e], rows[2 * e + 1], 0, 0).astype(BF16)

    hop = {}

    def send_back(e, h):
        for d in (2 * h, 2 * h + 1):
            pair[e, d].wait_recv()
        cols = pl.ds(h * half, half)
        both = acc[e, :, cols] + pair_in[e, :, cols].astype(F32)
        acc[e, 0:TILE, cols] = both[0:TILE]
        back_out[e, TILE:, cols] = both[TILE:].astype(BF16)
        for b in (6, 5, 7, 2, 4, 1, 3):
            block = pl.ds(b * TILE, TILE)
            hop[e, h, b] = remote(
                back_out.at[e, block, cols], back_in.at[e, block, cols], mate(b)
            )

    def back_over_ex(e):
        for h in range(2):
            for b in range(1, 8):
                hop[e, h, b].wait_recv()
        summed = acc[e, 0:TILE]
        for b in range(1, 8):
            summed += back_in[e, b * TILE : (b + 1) * TILE].astype(F32)
        summed = summed.astype(BF16)
        out, lane = iota((128, TILE), 0), iota((128, TILE), 1)
        fits = lane == (out // 16) * 2 + out % 2
        total = None
        for q in range(8):
            choose = onehot(fits & ((out // 2) % 8 == q))
            term = dot(choose, summed[:, q * eighth : (q + 1) * eighth], 1, 0)
            total = term if total is None else total + term
        ret_out[e] = total.astype(BF16)
        for k in range(1, PEERS):
            part = pl.ds(k * TILE, TILE)
            into = ret_in.at[pl.ds(e * 128 + k * TILE, TILE)]
            hop[e, k] = remote(ret_out.at[e, part], into, peer(k, -1))
        ret_in[e * 128 : e * 128 + TILE] = ret_out[e, 0:TILE]

    def combine():
        pick = []
        for e in range(2):
            m = matches(e)
            pick.append(m[0] + m[1])
        pick = jnp.concatenate(pick, axis=0)
        part_of = (iota((256, 16), 0) // 2) % 8
        chosen = [jnp.where(part_of == q, pick, 0.0).astype(BF16) for q in range(8)]
        for e in range(2):
            for k in range(1, PEERS):
                hop[e, k].wait_recv()
        for q in range(8):
            gtok_ref[:, q * eighth : (q + 1) * eighth] = dot(
                chosen[q], ret_in[...], 0, 0
            ).astype(BF16)

    tok_load.wait()
    cot_load.wait()
    build(0)
    pl.semaphore_wait(barrier, len(partners))
    over_ex(0)
    build(1)
    over_ex(1)
    form(0)
    across(0, 0)
    around(1, 0)
    around(0, 0)
    across(1, 0)
    share(0, 0, 0)
    share(1, 0, 0)
    form(1)
    across(2, 0)
    around(3, 0)
    across(3, 0)
    share(2, 0, 0)
    share(3, 0, 0)
    arrived(0, 0, 1, 0)
    around(0, 1)
    share(0, 1, 0)
    around(2, 0)
    for dz in (3, 1, 2):
        pass_across(1, dz)
    for dz in (3, 1, 2):
        pass_on(0, 0, dz)
    pass_on(1, 1, 0)
    arrived(2, 0, 1, 0)
    around(2, 1)
    share(2, 1, 0)
    for dz in (3, 1, 2):
        pass_across(3, dz)
    for dz in (3, 1, 2):
        pass_on(0, 1, dz)
    for dz in (3, 1, 2):
        pass_on(1, 1, dz)
    shared(0)
    for n in range(3):
        weights[n].wait()
    forward_inputs(0, 0)
    forward_inputs(0, 1)
    for dz in (3, 1, 2):
        pass_on(2, 0, dz)
    pass_on(3, 1, 0)
    shared(1)
    forward_grads(0, 0)
    forward_grads(0, 1)
    for d in range(2):
        input_grad(0, d)
    for dz in (3, 1, 2):
        pass_on(2, 1, dz)
    for d in range(2, 4):
        input_grad(0, d)
    for dz in (3, 1, 2):
        pass_on(3, 1, dz)
    send_back(0, 0)
    send_back(0, 1)
    for n in range(3, 6):
        weights[n].wait()
    shared(2)
    forward_inputs(1, 0)
    forward_inputs(1, 1)
    shared(3)
    forward_grads(1, 0)
    forward_grads(1, 1)
    input_grad(1, 0)
    input_grad(1, 1)
    input_grad(1, 2)
    input_grad(1, 3)
    weight_grad(0, 0)
    send_back(1, 0)
    send_back(1, 1)
    weight_grad(0, 1)
    back_over_ex(0)
    weight_grad(0, 2)
    weight_grad(1, 0)
    weight_grad(1, 1)
    back_over_ex(1)
    weight_grad(1, 2)
    combine()
    for copy in sent:
        copy.wait_send()


def write_kernel(a_ref, b_ref, c_ref, d_ref, a_hbm, b_hbm, c_hbm, d_hbm, sem):
    copies = [
        pltpu.make_async_copy(src, dst, sem.at[n])
        for n, (src, dst) in enumerate(
            ((a_ref, a_hbm), (b_ref, b_hbm), (c_ref, c_hbm), (d_ref, d_hbm))
        )
    ]
    for copy in copies:
        copy.start()
    for copy in copies:
        copy.wait()


def per_device(tokens, cotangent, route_weights, expert_ids, slot_ids, gate, up, down):
    local, width, hidden = gate.shape
    count = tokens.shape[0]
    total = BLOCKS * TILE
    vmem = pl.BlockSpec(memory_space=pltpu.VMEM)
    hbm = pl.BlockSpec(memory_space=pltpu.HBM)
    results = pl.pallas_call(
        main_kernel,
        out_shape=(
            pltpu.VMEM((count, width), BF16),
            pltpu.VMEM((local, width, hidden), BF16),
            pltpu.VMEM((local, width, hidden), BF16),
            pltpu.VMEM((local, hidden, width), BF16),
        ),
        in_specs=[hbm] * 2 + [vmem] * 3 + [hbm] * 3,
        out_specs=[vmem] * 4,
        scratch_shapes=[
            pltpu.VMEM((2 * count, width), BF16),
            pltpu.VMEM((4, total, width), BF16),
            pltpu.VMEM((local, total, hidden), BF16),
            pltpu.VMEM((local, total, hidden), BF16),
            pltpu.VMEM((local, total, hidden), BF16),
            pltpu.VMEM((2, total, hidden), F32),
            pltpu.VMEM((local, width, hidden), BF16),
            pltpu.VMEM((local, width, hidden), BF16),
            pltpu.VMEM((local, hidden, width), BF16),
            pltpu.VMEM((2, 128, width // 4), BF16),
            pltpu.VMEM((2, 128, width // 4), BF16),
            pltpu.VMEM((2, HALF_ROWS, width), F32),
            pltpu.VMEM((2, HALF_ROWS, width), BF16),
            pltpu.VMEM((2, HALF_ROWS, width), BF16),
            pltpu.VMEM((2, HALF_ROWS, width), BF16),
            pltpu.VMEM((2, HALF_ROWS, width), BF16),
            pltpu.VMEM((2, 128, width // 8), BF16),
            pltpu.VMEM((256, width // 8), BF16),
            pltpu.SemaphoreType.DMA((8,)),
            pltpu.SemaphoreType.DMA((150,)),
            pltpu.SemaphoreType.DMA((150,)),
        ],
        compiler_params=pltpu.CompilerParams(
            collective_id=0, has_side_effects=True, vmem_limit_bytes=46 * 1024 * 1024
        ),
    )(tokens, cotangent, route_weights.T, expert_ids.T, slot_ids.T, gate, up, down)
    return pl.pallas_call(
        write_kernel,
        out_shape=tuple(jax.ShapeDtypeStruct(a.shape, BF16) for a in results),
        in_specs=[vmem] * 4,
        out_specs=[hbm] * 4,
        scratch_shapes=[pltpu.SemaphoreType.DMA((4,))],
        compiler_params=pltpu.CompilerParams(vmem_limit_bytes=4 * 1024 * 1024),
    )(*results)


def solution(mesh):
    return jax.shard_map(
        per_device,
        mesh=mesh,
        in_specs=(
            P(("ex", "ey", "dp"), None),
            P(("ex", "ey", "dp"), None),
            P(("ex", "ey", "dp"), None),
            P(("ex", "ey", "dp"), None),
            P(("ex", "ey", "dp"), None),
            P("ex", None, ("ey", "dp")),
            P("ex", None, ("ey", "dp")),
            P("ex", ("ey", "dp"), None),
        ),
        out_specs=(
            P(("ex", "ey", "dp"), None),
            P("ex", None, ("ey", "dp")),
            P("ex", None, ("ey", "dp")),
            P("ex", ("ey", "dp"), None),
        ),
        check_vma=False,
    )
```

time: 189 us -> 60.2 us (0.32); the launches traced: 187 us -> 60.1 us
  waiting for transfers between devices: 84.8 us -> 0 us
  Pallas kernels: 0 us -> 59.4 us
  local copies, waits for them, and re-layouts: 47.5 us -> 0 us
  matrix products: 23.7 us -> 0 us
  starting transfers between devices: 22.9 us -> 0 us
  other arithmetic: 7.02 us -> 0 us
    all_to_all x3 -> x0, waiting for transfers between devices: 84.8 us -> none  [the longest x1 39.9 us: per_device(): lax.all_to_all(partial_all, ('ex', 'ey', 'dp'), split_axis=0, concat_axis...]
    pallas_call x0 -> x2, Pallas kernels: none -> 59.4 us  [the longest x1 54.7 us: per_device(): pl.pallas_call(main_kernel, out_shape=(pltpu.VMEM((count, width), BF16),...]
    dot_general x5 -> x0, matrix products: 23.7 us -> none  [the longest x1 7.76 us: per_device(): jnp.einsum('jrf,jdf->rjd', grad_pair, weight_pair, preferred_element_type...]
    all_to_all x3 -> x0, starting transfers between devices: 22.9 us -> none  [the longest x1 11.1 us: per_device(): lax.all_to_all(jnp.repeat(send_grad, shards, axis=0), ('ex', 'ey', 'dp'),...]
    reshape x5 -> x0, local copies, waits for them, and re-layouts: 19.8 us -> none  [the longest x2 12.7 us: per_device(): partial_all.reshape(ex_count * shards, capacity, local_count, model_width)]
    transpose x2 -> x0, local copies, waits for them, and re-layouts: 7.11 us -> none  [the longest x1 4.35 us: per_device(): jnp.transpose(rows_input, (1, 0, 2, 3))]
    broadcast_in_dim x4 -> x0, local copies, waits for them, and re-layouts: 7 us -> none  [the longest x1 3.41 us: per_device(): jnp.repeat(send_grad, shards, axis=0)]
    reduce_sum x4 -> x0, other arithmetic: 5.83 us -> none  [the longest x1 3.92 us: per_device(): jnp.sum(arrived.reshape(ex_count, shards, local_count, capacity, model_wi...]
  transfers between devices with their start and end apart: 3 -> 0, of which waited for: 3 -> 0; matrix products, arithmetic and copies ran while one was open for 15% -> 0% of each run, Pallas kernels for 0% -> 0%
where the time goes in v2:
time: 60.2 us; the launch traced here: 60.1 us
  Pallas kernels  59.4 us (99%)
  between operations  0.64 us (1%)
    pallas_call x1, Pallas kernels, per_device(): pl.pallas_call(main_kernel, out_shape=(pltpu.VMEM((count, width), BF16),...  54.7 us
    pallas_call x1, Pallas kernels, per_device(): pl.pallas_call(write_kernel, out_shape=tuple((jax.ShapeDtypeStruct(a.shap...  4.71 us

profile of v2, /device:TPU:0, one launch (start us, length us, event | category | flops | bytes accessed | tf_op | source)
XLA Modules:
  0.0 60.1 jit_solution(8889109594710895969)
XLA Ops:
  0.6 54.7 %shard_map.111 = (bf16[16,2048]{1,0:T(8,128)(2,1)S(1)}, bf16[2,2048,512]{2,1,0:T(8,128)(2,1)S(1)}, bf16[2,2048,512]{2,1,0:T(8,128)(2,1)S(1)}, bf16[2,512,2048]{2,1,0:T(8,128)(2,1)S(1)}) custom-call(bf16[16,2048]{1,0:T(8,128)(2,1)} %tok_hbm.1, bf16[16,2048]{1,0:T(8,128)(2,1)} %cot_hbm.1, f32[2,16]{1,0:T(2,128)} %bitcast.3, s32[2,16]{1,0:T(2,128)} %bitcast.4, ...), custom_call_target="tpu_custom_call" | custom-call | tf_op jit(solution)/shard_map/pallas_call | solution.py:380
  55.3 4.7 %shard_map.112 = (bf16[16,2048]{1,0:T(8,128)(2,1)}, bf16[2,2048,512]{2,1,0:T(8,128)(2,1)}, bf16[2,2048,512]{2,1,0:T(8,128)(2,1)}, bf16[2,512,2048]{2,1,0:T(8,128)(2,1)}) custom-call(bf16[16,2048]{1,0:T(8,128)(2,1)S(1)} %get-tuple-element.8.a_ref, bf16[2,2048,512]{2,1,0:T(8,128)(2,1)S(1)} %get-tuple-element.9.b_ref, ...), custom_call_target="tpu_custom_call" | custom-call | tf_op jit(solution)/shard_map/pallas_call | solution.py:417

commit v3 on v2

--- a/solution.py
+++ b/solution.py
@@ -97,54 +97,51 @@
         sent.append(copy)
         return copy
 
-    ids, slots, rw = ids_ref[...], slots_ref[...], rw_ref[...]
-    row = iota((128, 16), 0)
+    ids, slots, rw = [
+        jnp.concatenate([ref[...]] * 8, axis=1) for ref in (ids_ref, slots_ref, rw_ref)
+    ]
+    row, lane = iota((128, 128), 0), iota((128, 128), 1)
     piece = row // 16
     group = ((yh + piece // NX) % 2) * NX + (x + piece % NX) % NX
 
-    def matches(e):
-        expert, slot = group * 2 + e, row % 2
-        return [
-            jnp.where((ids[k : k + 1] == expert) & (slots[k : k + 1] == slot), 1.0, 0.0)
-            for k in range(2)
-        ]
+    def matches(e, k, also):
+        fits = (ids[k : k + 1] == group * 2 + e) & (slots[k : k + 1] == row % 2) & also
+        return jnp.where(fits, 1.0, 0.0)
+
+    def stacked(array, parts):
+        size = array.shape[1] // parts
+        return jnp.concatenate([array[:, n * size : (n + 1) * size] for n in range(parts)], axis=0)
 
     def build(e):
-        m = matches(e)
-        is_grad = (row // 2) % 2 == 1
-        any_match = m[0] + m[1]
+        is_grad = (row // 2) % 2
+        also = (lane // 32 == (row // 4) % 4) & ((lane // 16) % 2 == is_grad)
+        m = [matches(e, k, also) for k in range(2)]
         scale = jnp.sum(m[0] * rw[0:1] + m[1] * rw[1:2], axis=1, keepdims=True)
-        scale = jnp.where(is_grad[:, 0:1], scale, 1.0)
-        pick = jnp.concatenate(
-            [jnp.where(is_grad, 0.0, any_match), jnp.where(is_grad, any_match, 0.0)], axis=1
-        )
-        part_of = (iota((128, 32), 0) // 4) % 4
-        total = None
-        for q in range(4):
-            choose = jnp.where(part_of == q, pick, 0.0).astype(BF16)
-            term = dot(choose, tok_cot[:, q * quarter : (q + 1) * quarter], 1, 0)
-            total = term if total is None else total + term
-        send1[e] = (total * scale).astype(BF16)
+        scale = jnp.where(is_grad[:, 0:1] == 1, scale, 1.0)
+        picked = dot((m[0] + m[1]).astype(BF16), stacked(tok_cot[...], 4), 1, 0)
+        send1[e] = (picked * scale).astype(BF16)
 
     first = {}
 
     def over_ex(e):
         first[e] = []
-        for k in range(1, PEERS):
+        for k in (6, 2, 5, 7, 4, 1, 3):
             part = pl.ds(k * TILE, TILE)
             first[e].append(remote(send1.at[e, part], recv1.at[e, part], peer(k, 1)))
         recv1[e, 0:TILE] = send1[e, 0:TILE]
 
+    regroup = onehot(
+        lane == ((row % 16) // 2) * 16 + (row // 32) * 4 + ((row // 16) % 2) * 2 + row % 2
+    )
+
     def form(e):
         for copy in first[e]:
             copy.wait_recv()
-        out, lane = iota((32, 128), 0), iota((32, 128), 1)
-        source = ((out % 16) // 2) * 16 + (out // 16) * 2 + out % 2
+        block = dot(regroup, recv1[e], 1, 0).astype(BF16)
         for q in range(4):
-            block = dot(onehot(lane == source + 4 * q), recv1[e], 1, 0).astype(BF16)
             cols = slice(q * quarter, (q + 1) * quarter)
-            rows[2 * e, 0:TILE, cols] = block[0:TILE]
-            rows[2 * e + 1, 0:TILE, cols] = block[TILE:]
+            rows[2 * e, 0:TILE, cols] = block[q * 32 : q * 32 + 16]
+            rows[2 * e + 1, 0:TILE, cols] = block[q * 32 + 16 : q * 32 + 32]
 
     arrive = {}
 
@@ -234,6 +231,8 @@
                 back_out.at[e, block, cols], back_in.at[e, block, cols], mate(b)
             )
 
+    ungroup = onehot(lane == ((row // 2) % 8) * 16 + (row // 16) * 2 + row % 2)
+
     def back_over_ex(e):
         for h in range(2):
             for b in range(1, 8):
@@ -242,35 +241,24 @@
         for b in range(1, 8):
             summed += back_in[e, b * TILE : (b + 1) * TILE].astype(F32)
         summed = summed.astype(BF16)
-        out, lane = iota((128, TILE), 0), iota((128, TILE), 1)
-        fits = lane == (out // 16) * 2 + out % 2
-        total = None
-        for q in range(8):
-            choose = onehot(fits & ((out // 2) % 8 == q))
-            term = dot(choose, summed[:, q * eighth : (q + 1) * eighth], 1, 0)
-            total = term if total is None else total + term
-        ret_out[e] = total.astype(BF16)
-        for k in range(1, PEERS):
+        ret_out[e] = dot(ungroup, stacked(summed, 8), 1, 0).astype(BF16)
+        for k in (6, 2, 5, 7, 4, 1, 3):
             part = pl.ds(k * TILE, TILE)
             into = ret_in.at[pl.ds(e * 128 + k * TILE, TILE)]
             hop[e, k] = remote(ret_out.at[e, part], into, peer(k, -1))
         ret_in[e * 128 : e * 128 + TILE] = ret_out[e, 0:TILE]
 
     def combine():
-        pick = []
-        for e in range(2):
-            m = matches(e)
-            pick.append(m[0] + m[1])
-        pick = jnp.concatenate(pick, axis=0)
-        part_of = (iota((256, 16), 0) // 2) % 8
-        chosen = [jnp.where(part_of == q, pick, 0.0).astype(BF16) for q in range(8)]
+        here = lane // 16 == (row // 2) % 8
+        pick = jnp.concatenate(
+            [(matches(e, 0, here) + matches(e, 1, here)).astype(BF16) for e in range(2)], axis=0
+        )
         for e in range(2):
             for k in range(1, PEERS):
                 hop[e, k].wait_recv()
+        out = dot(pick, ret_in[...], 0, 0).astype(BF16)
         for q in range(8):
-            gtok_ref[:, q * eighth : (q + 1) * eighth] = dot(
-                chosen[q], ret_in[...], 0, 0
-            ).astype(BF16)
+            gtok_ref[:, q * eighth : (q + 1) * eighth] = out[q * 16 : (q + 1) * 16]
 
     tok_load.wait()
     cot_load.wait()
@@ -343,11 +331,11 @@
     input_grad(1, 1)
     input_grad(1, 2)
     input_grad(1, 3)
-    weight_grad(0, 0)
     send_back(1, 0)
     send_back(1, 1)
+    weight_grad(0, 0)
+    back_over_ex(0)
     weight_grad(0, 1)
-    back_over_ex(0)
     weight_grad(0, 2)
     weight_grad(1, 0)
     weight_grad(1, 1)

time: 60.2 us -> 59.5 us (0.988)
  Pallas kernels: 59.4 us -> 58.7 us
    pallas_call x1, Pallas kernels: 54.7 us -> 54 us  [per_device(): pl.pallas_call(main_kernel, out_shape=(pltpu.VMEM((count, width), BF16),...]
where the time goes in v3:
time: 59.5 us; the launch traced here: 59.4 us
  Pallas kernels  58.7 us (99%)
  between operations  0.64 us (1%)
    pallas_call x1, Pallas kernels, per_device(): pl.pallas_call(main_kernel, out_shape=(pltpu.VMEM((count, width), BF16),...  54 us
    pallas_call x1, Pallas kernels, per_device(): pl.pallas_call(write_kernel, out_shape=tuple((jax.ShapeDtypeStruct(a.shap...  4.71 us

profile of v3, /device:TPU:0, one launch (start us, length us, event | category | flops | bytes accessed | tf_op | source)
XLA Modules:
  0.0 59.4 jit_solution(13669006460829384581)
XLA Ops:
  0.6 54.0 %shard_map.111 = (bf16[16,2048]{1,0:T(8,128)(2,1)S(1)}, bf16[2,2048,512]{2,1,0:T(8,128)(2,1)S(1)}, bf16[2,2048,512]{2,1,0:T(8,128)(2,1)S(1)}, bf16[2,512,2048]{2,1,0:T(8,128)(2,1)S(1)}) custom-call(bf16[16,2048]{1,0:T(8,128)(2,1)} %tok_hbm.1, bf16[16,2048]{1,0:T(8,128)(2,1)} %cot_hbm.1, f32[2,16]{1,0:T(2,128)} %bitcast.3, s32[2,16]{1,0:T(2,128)} %bitcast.4, ...), custom_call_target="tpu_custom_call" | custom-call | tf_op jit(solution)/shard_map/pallas_call | solution.py:368
  54.7 4.7 %shard_map.112 = (bf16[16,2048]{1,0:T(8,128)(2,1)}, bf16[2,2048,512]{2,1,0:T(8,128)(2,1)}, bf16[2,2048,512]{2,1,0:T(8,128)(2,1)}, bf16[2,512,2048]{2,1,0:T(8,128)(2,1)}) custom-call(bf16[16,2048]{1,0:T(8,128)(2,1)S(1)} %get-tuple-element.8.a_ref, bf16[2,2048,512]{2,1,0:T(8,128)(2,1)S(1)} %get-tuple-element.9.b_ref, ...), custom_call_target="tpu_custom_call" | custom-call | tf_op jit(solution)/shard_map/pallas_call | solution.py:405

commit v4 on v3

--- a/solution.py
+++ b/solution.py
@@ -337,9 +337,9 @@
     back_over_ex(0)
     weight_grad(0, 1)
     weight_grad(0, 2)
+    back_over_ex(1)
     weight_grad(1, 0)
     weight_grad(1, 1)
-    back_over_ex(1)
     weight_grad(1, 2)
     combine()
     for copy in sent:

time: 59.5 us -> 59.5 us (level)
  no operation moved by 1% of the time
where the time goes in v4:
time: 59.5 us; the launch traced here: 59.4 us
  Pallas kernels  58.7 us (99%)
  between operations  0.64 us (1%)
    pallas_call x1, Pallas kernels, per_device(): pl.pallas_call(main_kernel, out_shape=(pltpu.VMEM((count, width), BF16),...  54 us
    pallas_call x1, Pallas kernels, per_device(): pl.pallas_call(write_kernel, out_shape=tuple((jax.ShapeDtypeStruct(a.shap...  4.71 us

profile of v4, /device:TPU:0, one launch (start us, length us, event | category | flops | bytes accessed | tf_op | source)
XLA Modules:
  0.0 59.4 jit_solution(17530960687542920049)
XLA Ops:
  0.6 54.0 %shard_map.111 = (bf16[16,2048]{1,0:T(8,128)(2,1)S(1)}, bf16[2,2048,512]{2,1,0:T(8,128)(2,1)S(1)}, bf16[2,2048,512]{2,1,0:T(8,128)(2,1)S(1)}, bf16[2,512,2048]{2,1,0:T(8,128)(2,1)S(1)}) custom-call(bf16[16,2048]{1,0:T(8,128)(2,1)} %tok_hbm.1, bf16[16,2048]{1,0:T(8,128)(2,1)} %cot_hbm.1, f32[2,16]{1,0:T(2,128)} %bitcast.3, s32[2,16]{1,0:T(2,128)} %bitcast.4, ...), custom_call_target="tpu_custom_call" | custom-call | tf_op jit(solution)/shard_map/pallas_call | solution.py:368
  54.7 4.7 %shard_map.112 = (bf16[16,2048]{1,0:T(8,128)(2,1)}, bf16[2,2048,512]{2,1,0:T(8,128)(2,1)}, bf16[2,2048,512]{2,1,0:T(8,128)(2,1)}, bf16[2,512,2048]{2,1,0:T(8,128)(2,1)}) custom-call(bf16[16,2048]{1,0:T(8,128)(2,1)S(1)} %get-tuple-element.8.a_ref, bf16[2,2048,512]{2,1,0:T(8,128)(2,1)S(1)} %get-tuple-element.9.b_ref, ...), custom_call_target="tpu_custom_call" | custom-call | tf_op jit(solution)/shard_map/pallas_call | solution.py:405
